TPU v7x, 32 devices: a whole 2x2x4 slice. The times are simulated.
32 devices in a mesh: gx: 8 (over y, x, core), gy: 4 (over z).
Axes of the slice: x: 2, y: 2, z: 4, core: 2. Of those that a mesh axis runs over, the one named last changes fastest.
Arguments:
- velocity: float32 [3, 128, 64, 512], P(None, 'gx', 'gy'), may hold values from -6 to 6
- stress: float32 [6, 128, 64, 512], P(None, 'gx', 'gy'), may hold values from -6 to 6
- pier_velocity: float32 [128, 16], P('gx', 'gy'), may hold values from -6 to 6
- buoyancy: float32 [128, 64, 512], P('gx', 'gy'), may hold values from 0.5 to 2
- layer: int32 [128], P('gx'), may hold values from 0 to 7, as said below
- lame_table: float32 [8], replicated, may hold values from 0.3 to 1.2
- shear_table: float32 [8], replicated, may hold values from 0.2 to 0.8
- relax_table: float32 [8], replicated, may hold values from 0.6 to 0.95
- impedance: float32 [16], P('gy'), may hold values from 0.5 to 2
- footprint: int32 [16, 16], replicated, may hold values from 0 to 32767, as said below
- damp_inverse: float32 [128, 128], replicated
Outputs:
- velocity_out: float32 [3, 128, 64, 512], P(None, 'gx', 'gy')
- stress_out: float32 [6, 128, 64, 512], P(None, 'gx', 'gy')
- pier_out: float32 [128, 16], P('gx', 'gy')
Inputs may be any that keep to these rules, and one draw needn't show every extreme that they name: `footprint`: row p lists the 16 cells of a square of 4 by 4 cells, row by row; squares may intersect and lie anywhere in the plane. `layer`: non-decreasing along depth; the first cell is in layer 0 and the last in layer 7.
All inputs are finite; a program needn't handle non-finite values.
Results may differ from a plain program's by a relative error of at most 0.00011.
Values sent between devices are 32-bit elements; how exact they have to be, the bound alone decides.
A program may use at most 192 MiB of HBM per device.

v0:
```python
import jax
import jax.numpy as jnp
from jax import lax
from jax.sharding import PartitionSpec as P

STEPS = 2
FOOT = 16
grid_ratio = 0.25
soil_gain = 0.2
pier_gain = 0.5


def extended(cells, sides, width):
    for axis, dim in sides:
        count = lax.axis_size(axis)
        ends = count - 1
        head = lax.slice_in_dim(cells, 0, width, axis=dim)
        tail = lax.slice_in_dim(cells, cells.shape[dim] - width, cells.shape[dim], axis=dim)
        cells = jnp.concatenate(
            [
                lax.ppermute(tail, axis, [(i, (i + 1) % count) for i in range(ends)]),
                cells,
                lax.ppermute(head, axis, [((i + 1) % count, i) for i in range(ends)]),
            ],
            axis=dim,
        )
    return cells


def forward_diff(padded, along):
    center = padded[1:-1, 1:-1, 1:-1]
    if along == 0:
        return padded[2:, 1:-1, 1:-1] - center
    if along == 1:
        return padded[1:-1, 2:, 1:-1] - center
    return padded[1:-1, 1:-1, 2:] - center


def backward_diff(padded, along):
    center = padded[1:-1, 1:-1, 1:-1]
    if along == 0:
        return center - padded[:-2, 1:-1, 1:-1]
    if along == 1:
        return center - padded[1:-1, :-2, 1:-1]
    return center - padded[1:-1, 1:-1, :-2]


def move_velocity(velocity, padded, buoyancy):
    scaled = grid_ratio * buoyancy
    first = velocity[0] + scaled * (
        backward_diff(padded[0], 2) + forward_diff(padded[3], 1) + forward_diff(padded[4], 0)
    )
    second = velocity[1] + scaled * (
        forward_diff(padded[3], 2) + backward_diff(padded[1], 1) + forward_diff(padded[5], 0)
    )
    third = velocity[2] + scaled * (
        forward_diff(padded[4], 2) + forward_diff(padded[5], 1) + backward_diff(padded[2], 0)
    )
    return jnp.stack([first, second, third])


def move_stress(stress, padded, lame_first, shear_mod, relax):
    strain_x = forward_diff(padded[0], 2)
    strain_y = forward_diff(padded[1], 1)
    strain_z = forward_diff(padded[2], 0)
    modulus = lame_first + 2.0 * shear_mod
    normal_x = relax * stress[0] + grid_ratio * (
        modulus * strain_x + lame_first * (strain_y + strain_z)
    )
    normal_y = relax * stress[1] + grid_ratio * (
        modulus * strain_y + lame_first * (strain_x + strain_z)
    )
    normal_z = relax * stress[2] + grid_ratio * (
        modulus * strain_z + lame_first * (strain_x + strain_y)
    )
    shear_xy = relax * stress[3] + grid_ratio * shear_mod * (
        backward_diff(padded[0], 1) + backward_diff(padded[1], 2)
    )
    shear_xz = relax * stress[4] + grid_ratio * shear_mod * (
        backward_diff(padded[0], 0) + backward_diff(padded[2], 2)
    )
    shear_yz = relax * stress[5] + grid_ratio * shear_mod * (
        backward_diff(padded[1], 0) + backward_diff(padded[2], 1)
    )
    return jnp.stack([normal_x, normal_y, normal_z, shear_xy, shear_xz, shear_yz])


def layer_values(layer, table):
    levels = jnp.arange(table.shape[0], dtype=jnp.int32)
    onehot = (layer[:, None] == levels[None, :]).astype(table.dtype)
    return jnp.sum(onehot * table[None, :], axis=1)[:, None, None]


def with_faces(fields):
    padded = extended(fields, (("gx", 1), ("gy", 2)), 1)
    return jnp.pad(padded, ((0, 0), (0, 0), (0, 0), (1, 1)))


def footprint_matches(cell_ids, footprint):
    piers = footprint.shape[0]
    equal = (cell_ids[:, None] == footprint.reshape(-1)[None, :]).astype(jnp.float32)
    return jnp.sum(equal.reshape(cell_ids.shape[0], piers, FOOT), axis=2)


def damp_columns(velocity, inverse):
    pencils = lax.all_to_all(velocity, "gx", split_axis=3, concat_axis=1, tiled=True)
    shape = pencils.shape
    flat = pencils.reshape(shape[0], shape[1], shape[2] * shape[3])
    damped = jnp.einsum("zk,fkm->fzm", inverse, flat, precision=lax.Precision.HIGHEST).reshape(
        shape
    )
    return lax.all_to_all(damped, "gx", split_axis=1, concat_axis=3, tiled=True)


def body(
    velocity,
    stress,
    pier_velocity,
    buoyancy,
    layer,
    lame_table,
    shear_table,
    relax_table,
    impedance,
    footprint,
    damp_inverse,
):
    depth_cells, side_cells, line_cells = (velocity.shape[1], velocity.shape[2], velocity.shape[3])
    own_piers = pier_velocity.shape[1]
    lame_first = layer_values(layer, lame_table)
    shear_mod = layer_values(layer, shear_table)
    relax = layer_values(layer, relax_table)
    row_start = lax.axis_index("gy") * side_cells
    cell_ids = row_start * line_cells + jnp.arange(side_cells * line_cells, dtype=jnp.int32)
    selector = footprint_matches(cell_ids, footprint)
    own_foot = lax.dynamic_slice_in_dim(footprint, lax.axis_index("gy") * own_piers, own_piers, 0)
    for time_step in range(STEPS):
        padded = with_faces(stress)
        velocity = move_velocity(velocity, padded, buoyancy)
        vertical = velocity[2].reshape(depth_cells, side_cells * line_cells)
        piece = lax.all_gather(velocity[2], "gy", axis=1, tiled=True)
        count = piece.shape[1]
        piece_ids = jnp.arange(count * line_cells, dtype=jnp.int32)
        picks = footprint_matches(piece_ids, own_foot)
        flat = piece.reshape(depth_cells, count * line_cells)
        summed = jnp.dot(
            flat, picks, precision=lax.Precision.HIGHEST, preferred_element_type=jnp.float32
        )
        mean_speed = summed / FOOT
        force = impedance[None, :] * (pier_velocity - mean_speed)
        pier_velocity = pier_velocity - pier_gain * force
        all_force = lax.all_gather(force, "gy", axis=1, tiled=True)
        pushed = jnp.dot(
            all_force,
            selector.T,
            precision=lax.Precision.HIGHEST,
            preferred_element_type=jnp.float32,
        )
        vertical = vertical + soil_gain * pushed
        velocity = jnp.stack(
            [velocity[0], velocity[1], vertical.reshape(depth_cells, side_cells, line_cells)]
        )
        velocity = damp_columns(velocity, damp_inverse)
        padded = with_faces(velocity)
        stress = move_stress(stress, padded, lame_first, shear_mod, relax)
    return (velocity, stress, pier_velocity)


def solution(mesh):
    placed = (
        P(None, "gx", "gy", None),
        P(None, "gx", "gy", None),
        P("gx", "gy"),
        P("gx", "gy", None),
        P("gx"),
        P(),
        P(),
        P(),
        P("gy"),
        P(),
        P(),
    )
    return jax.shard_map(
        body,
        mesh=mesh,
        in_specs=placed,
        out_specs=(P(None, "gx", "gy", None), P(None, "gx", "gy", None), P("gx", "gy")),
        check_vma=False,
    )
```

profile of v0, /device:TPU:11, one launch (start us, length us, event | category | flops | bytes accessed | tf_op | source)
XLA Modules:
  0.0 499.5 jit_solution(11973510932062096920)
XLA Ops:
  8.3 3.7 collective-permute-start
  16.9 3.0 collective-permute-done.1
  20.3 3.2 collective-permute-start.2
  28.5 3.2 collective-permute-done.3
  31.7 4.2 select_maximum_fusion.4
  47.9 5.0 fusion.58
  52.8 31.2 %all-gather.5.cloned.1.call-done = f32[16,64,512]{2,1,0:T(8,128)} async-done(((f32[16,16,512]{2,1,0:T(8,128)}), f32[16,64,512]{2,1,0:T(8,128)}) %all-gather.5.cloned.1.call-update) | async-done | bytes 2097168 | tf_op jit(solution)/shard_map/all_gather | solution.py:141
  89.5 9.2 %all-gather = f32[4,4,16]{2,1,0:T(4,128)S(1)} all-gather(f32[1,4,16]{2,1,0:T(4,128)S(1)} %bitcast.214), channel_id=1, replica_groups=mesh['gx'=8,'gy'=4] {'gy'}, dimensions={0}, use_global_device_ids=true | all-gather | bytes 1280 | tf_op jit(solution)/shard_map/all_gather | solution.py:152
  99.9 8.8 %copy.50 = f32[3,16,16,512]{2,1,0,3:T(8,128)} copy(f32[3,16,16,512]{3,2,1,0:T(8,128)S(1)} %pad_maximum_fusion) | data formatting | bytes 3145728 | tf_op jit(solution)/shard_map/stack | solution.py:160
  108.7 8.9 %reshape.89 = f32[8,1,49152]{2,1,0:T(1,128)S(1)} reshape(f32[512,3,16,16]{3,2,1,0:T(8,128)} %bitcast.186) | data formatting | bytes 3145728
  117.5 26.2 %all_to_all.66 = f32[8,1,49152]{2,1,0:T(1,128)S(1)} all-to-all(f32[8,1,49152]{2,1,0:T(1,128)S(1)} %reshape.89), channel_id=1, replica_groups=mesh['gx'=8,'gy'=4] {'gx'}, dimensions={0} | all-to-all | bytes 3145728 | tf_op jit(solution)/shard_map/all_to_all | solution.py:106
  144.3 4.4 reduce
  148.8 8.7 %reshape.90 = f32[512,3,16,16]{3,2,1,0:T(8,128)} reshape(f32[8,49152]{1,0:T(8,128)S(1)} %reduce) | data formatting | bytes 3145728
  157.5 8.1 %copy.51 = f32[3,16,16,8,64]{4,2,1,3,0:T(8,128)S(1)} copy(f32[3,16,16,8,64]{2,1,0,4,3:T(8,128)} %bitcast.188) | data formatting | bytes 3145728 | tf_op jit(solution)/shard_map/all_to_all | solution.py:106
  167.4 5.2 %fusion.65 = f32[3,1024,128]{2,1,0:T(8,128)} fusion(f32[3,128,1024]{2,1,0:T(8,128)} %reshape.79, f32[128,128]{1,0:T(8,128)S(1)} %copy-done), kind=kOutput, calls=%fused_computation.160 | convolution fusion | flops 603979776 | bytes 3211264 | tf_op jit(solution)/shard_map/zk,fkm->fzm/dot_general | solution.py:109
  175.2 3.0 reshape.91
  178.2 24.5 %all_to_all.67 = f32[8,1,49152]{2,1,0:T(1,128)S(1)} all-to-all(f32[8,1,49152]{2,1,0:T(1,128)} %reshape.91), channel_id=1, replica_groups=mesh['gx'=8,'gy'=4] {'gx'}, dimensions={0} | all-to-all | bytes 3145728 | tf_op jit(solution)/shard_map/all_to_all | solution.py:112
  202.7 6.2 %reduce.1 = f32[8,49152]{1,0:T(8,128)} reduce(f32[8,1,49152]{2,1,0:T(1,128)S(1)} %all_to_all.67, f32[]{:T(128)} %broadcast.158), dimensions={1}, to_apply=%all_to_all.51.reduce_sub_computation | reduce | bytes 3145732 | tf_op jit(solution)/shard_map/all_to_all | solution.py:112
  211.5 3.5 copy.56
  215.0 3.8 all_to_all.54
  219.8 3.6 collective-permute-start.4
  227.0 3.3 collective-permute-done.5
  230.5 3.8 collective-permute-start.6
  236.4 3.4 collective-permute-done.7
  253.2 3.2 collective-permute-start.8
  259.1 5.3 %collective-permute-done.9 = f32[6,1,16,512]{3,2,1,0:T(8,128)S(1)} collective-permute-done((f32[6,1,16,512]{3,2,1,0:T(8,128)S(1)}, f32[6,1,16,512]{3,2,1,0:T(8,128)S(1)}, u32[]{:S(2)}, u32[]{:S(2)}) %collective-permute-start.9) | collective-permute-done | bytes 196640 | tf_op jit(solution)/shard_map/ppermute | solution.py:23
  267.5 4.2 collective-permute-start.11
  277.3 5.8 %select_maximum_fusion = f32[6,18,18,514]{3,2,1,0:T(8,128)S(1)} fusion(f32[6,18,1,512]{3,2,1,0:T(1,128)} %collective-permute-done.11, f32[6,18,1,512]{3,2,1,0:T(1,128)} %collective-permute-done.10, f32[6,1,16,512]{3,2,1,0:T(8,128)} %copy-done.25, f32[6,16,16,512]{3,2,1,0:T(8,128)S(1)} %copy-done.2, f32[6,1,16,512]{3,2,1,0:T(8,128)S(1)} %collective-permute-done.8), kind=kLoop, calls=%fused_computation.9 | loop fusion | flops 11990592 | bytes 7978176 | tf_op jit(solution)/shard_map/concatenate | solution.py:19
  291.8 3.0 copy.57
  298.2 5.7 %fusion.35 = (f32[1,16,16,512]{3,2,1,0:T(8,128)S(1)}, f32[1,16,16,512]{3,2,1,0:T(8,128)}) fusion(f32[16,16,512]{2,1,0:T(8,128)} %squeeze.117, f32[18,18,514]{2,1,0:T(8,128)S(1)} %get-tuple-element.21, f32[18,18,514]{2,1,0:T(8,128)} %get-tuple-element.22, f32[18,18,514]{2,1,0:T(8,128)} %get-tuple-element.18, f32[16,16,512]{2,1,0:T(8,128)S(1)} %copy-done.5, ...), kind=kLoop, calls=%fused_computation.92 | loop fusion | flops 1966080 | bytes 8388608 | tf_op jit(solution)/shard_map/stack | solution.py:59
  303.9 24.7 %all-gather.7.cloned.1.call-done = f32[16,64,512]{2,1,0:T(8,128)} async-done(((f32[16,16,512]{2,1,0:T(8,128)}), f32[16,64,512]{2,1,0:T(8,128)}) %all-gather.7.cloned.1.call-update) | async-done | bytes 2097168 | tf_op jit(solution)/shard_map/all_gather | solution.py:141
  331.5 3.2 multiply_subtract_fusion
  334.7 9.2 %all-gather.1 = f32[4,4,16]{2,1,0:T(4,128)S(1)} all-gather(f32[1,4,16]{2,1,0:T(4,128)S(1)} %bitcast.215), channel_id=1, replica_groups=mesh['gx'=8,'gy'=4] {'gy'}, dimensions={0}, use_global_device_ids=true | all-gather | bytes 1280 | tf_op jit(solution)/shard_map/all_gather | solution.py:152
  345.1 8.8 %copy.59 = f32[3,16,16,512]{2,1,0,3:T(8,128)} copy(f32[3,16,16,512]{3,2,1,0:T(8,128)S(1)} %pad_maximum_fusion.1) | data formatting | bytes 3145728 | tf_op jit(solution)/shard_map/stack | solution.py:160
  353.9 8.9 %reshape.93 = f32[8,1,49152]{2,1,0:T(1,128)S(1)} reshape(f32[512,3,16,16]{3,2,1,0:T(8,128)} %bitcast.187) | data formatting | bytes 3145728
  362.7 26.4 %all_to_all.68 = f32[8,1,49152]{2,1,0:T(1,128)S(1)} all-to-all(f32[8,1,49152]{2,1,0:T(1,128)S(1)} %reshape.93), channel_id=1, replica_groups=mesh['gx'=8,'gy'=4] {'gx'}, dimensions={0} | all-to-all | bytes 3145728 | tf_op jit(solution)/shard_map/all_to_all | solution.py:106
  389.2 4.4 reduce.2
  393.6 8.7 %reshape.94 = f32[512,3,16,16]{3,2,1,0:T(8,128)} reshape(f32[8,49152]{1,0:T(8,128)S(1)} %reduce.2) | data formatting | bytes 3145728
  402.3 8.1 %copy.60 = f32[3,16,16,8,64]{4,2,1,3,0:T(8,128)S(1)} copy(f32[3,16,16,8,64]{2,1,0,4,3:T(8,128)} %bitcast.189) | data formatting | bytes 3145728 | tf_op jit(solution)/shard_map/all_to_all | solution.py:106
  412.2 5.2 %fusion.63 = f32[3,1024,128]{2,1,0:T(8,128)} fusion(f32[3,128,1024]{2,1,0:T(8,128)} %reshape.82, f32[128,128]{1,0:T(8,128)S(1)} %copy-done), kind=kOutput, calls=%fused_computation.158 | convolution fusion | flops 603979776 | bytes 3211264 | tf_op jit(solution)/shard_map/zk,fkm->fzm/dot_general | solution.py:109
  419.8 3.0 reshape.95
  422.8 24.5 %all_to_all.69 = f32[8,1,49152]{2,1,0:T(1,128)S(1)} all-to-all(f32[8,1,49152]{2,1,0:T(1,128)} %reshape.95), channel_id=1, replica_groups=mesh['gx'=8,'gy'=4] {'gx'}, dimensions={0} | all-to-all | bytes 3145728 | tf_op jit(solution)/shard_map/all_to_all | solution.py:112
  447.3 6.2 %reduce.3 = f32[8,49152]{1,0:T(8,128)} reduce(f32[8,1,49152]{2,1,0:T(1,128)S(1)} %all_to_all.69, f32[]{:T(128)} %broadcast.158), dimensions={1}, to_apply=%all_to_all.58.reduce_sub_computation | reduce | bytes 3145732 | tf_op jit(solution)/shard_map/all_to_all | solution.py:112
  456.1 3.5 copy.64
  462.5 3.6 collective-permute-start.12
  468.2 4.7 collective-permute-done.13
  473.1 3.8 collective-permute-start.14
  479.1 3.3 collective-permute-done.15
  (158 shorter events, 109.4 us)
Async XLA Ops:
  7.2 160.2 %copy-start = (f32[128,128]{1,0:T(8,128)S(1)}, f32[128,128]{1,0:T(8,128)}, u32[]{:S(2)}) copy-start(f32[128,128]{1,0:T(8,128)} %param.21) | copy-start | bytes 196612
  7.2 76.8 %all-gather.5.cloned.1.call-start = ((), (), s32[]{:S(2)}) async-start(), calls=%async_computation.4 | async-start | bytes 2621440 | tf_op jit(solution)/shard_map/all_gather | solution.py:141
  8.3 6.3 %collective-permute-start = (f32[6,1,16,512]{3,2,1,0:T(8,128)S(1)}, f32[6,1,16,512]{3,2,1,0:T(8,128)S(1)}, u32[]{:S(2)}, u32[]{:S(2)}) collective-permute-start(f32[6,1,16,512]{3,2,1,0:T(8,128)S(1)} %get-tuple-element.48), channel_id=1, source_target_pairs={{0,4},{4,8},{8,12},{12,16},{16,20},{20,24},{24,28},{1,5},{5,9},{9,... | collective-permute-start | bytes 589832 | tf_op jit(solution)/shard_map/ppermute | solution.py:21
  12.0 7.9 %collective-permute-start.1 = (f32[6,1,16,512]{3,2,1,0:T(8,128)S(1)}, f32[6,1,16,512]{3,2,1,0:T(8,128)S(1)}, u32[]{:S(2)}, u32[]{:S(2)}) collective-permute-start(f32[6,1,16,512]{3,2,1,0:T(8,128)S(1)} %get-tuple-element.47), channel_id=1, source_target_pairs={{4,0},{8,4},{12,8},{16,12},{20,16},{24,20},{28,24},{5,1},{9,5},{13... | collective-permute-start | bytes 589832 | tf_op jit(solution)/shard_map/ppermute | solution.py:23
  20.3 8.2 %collective-permute-start.2 = (f32[6,18,1,512]{3,2,1,0:T(1,128)S(1)}, f32[6,18,1,512]{3,2,1,0:T(1,128)S(1)}, u32[]{:S(2)}, u32[]{:S(2)}) collective-permute-start(f32[6,18,1,512]{3,2,1,0:T(1,128)S(1)} %get-tuple-element.32), channel_id=1, source_target_pairs={{0,1},{1,2},{2,3},{4,5},{5,6},{6,7},{8,9},{9,10},{10,11},{12,13},{... | collective-permute-start | bytes 663560 | tf_op jit(solution)/shard_map/ppermute | solution.py:21
  23.5 8.2 %collective-permute-start.3 = (f32[6,18,1,512]{3,2,1,0:T(1,128)S(1)}, f32[6,18,1,512]{3,2,1,0:T(1,128)S(1)}, u32[]{:S(2)}, u32[]{:S(2)}) collective-permute-start(f32[6,18,1,512]{3,2,1,0:T(1,128)S(1)} %get-tuple-element.33), channel_id=1, source_target_pairs={{1,0},{2,1},{3,2},{5,4},{6,5},{7,6},{9,8},{10,9},{11,10},{13,12},{... | collective-permute-start | bytes 663560 | tf_op jit(solution)/shard_map/ppermute | solution.py:23
  35.9 1.8 copy-start.4
  37.8 3.1 copy-start.27
  40.6 288.0 %all-gather.7.cloned.1.call-start = ((), (), s32[]{:S(2)}) async-start(), calls=%async_computation.5 | async-start | bytes 2621440 | tf_op jit(solution)/shard_map/all_gather | solution.py:141
  40.8 7.0 %copy-start.7 = (f32[18,18,514]{2,1,0:T(8,128)S(1)}, f32[18,18,514]{2,1,0:T(8,128)}, u32[]{:S(2)}) copy-start(f32[18,18,514]{2,1,0:T(8,128)} %get-tuple-element.28) | copy-start | bytes 1998436
  45.5 53.2 %copy-start.8 = (f32[8192,16]{0,1:T(8,128)}, f32[8192,16]{0,1:T(8,128)S(1)}, u32[]{:S(2)}) copy-start(f32[8192,16]{0,1:T(8,128)S(1)} %convert_reduce_fusion) | copy-start | bytes 1572868
  84.0 2.9 copy-start.11
  84.0 2.9 copy-start.28
  84.0 2.9 copy-start.29
  86.9 11.9 %copy-start.15 = (f32[2,8,16,512]{3,1,2,0:T(8,128)S(1)}, f32[2,8,16,512]{3,1,2,0:T(8,128)}, u32[]{:S(2)}) copy-start(f32[2,8,16,512]{3,1,2,0:T(8,128)} %copy.69) | copy-start | bytes 1572868
  86.9 12.8 %copy-start.17 = (f32[1,16,16,512]{3,2,1,0:T(8,128)S(1)}, f32[1,16,16,512]{3,2,1,0:T(8,128)}, u32[]{:S(2)}) copy-start(f32[1,16,16,512]{3,2,1,0:T(8,128)} %get-tuple-element.40) | copy-start | bytes 1572868
  86.9 12.8 %copy-start.18 = (f32[1,16,16,512]{3,2,1,0:T(8,128)S(1)}, f32[1,16,16,512]{3,2,1,0:T(8,128)}, u32[]{:S(2)}) copy-start(f32[1,16,16,512]{3,2,1,0:T(8,128)} %get-tuple-element.41) | copy-start | bytes 1572868
  215.0 8.3 %copy-start.30 = (f32[8]{0:T(128)S(1)}, f32[8]{0:T(128)}, u32[]{:S(2)}) copy-start(f32[8]{0:T(128)} %param.18) | copy-start | bytes 100
  215.0 8.3 %copy-start.31 = (s32[16]{0:T(128)S(1)}, s32[16]{0:T(128)}, u32[]{:S(2)}) copy-start(s32[16]{0:T(128)} %param.15) | copy-start | bytes 196
  215.0 8.3 %copy-start.32 = (f32[8]{0:T(128)S(1)}, f32[8]{0:T(128)}, u32[]{:S(2)}) copy-start(f32[8]{0:T(128)} %param.17) | copy-start | bytes 100
  215.0 8.3 %copy-start.33 = (f32[8]{0:T(128)S(1)}, f32[8]{0:T(128)}, u32[]{:S(2)}) copy-start(f32[8]{0:T(128)} %param.16) | copy-start | bytes 100
  219.8 5.6 %collective-permute-start.4 = (f32[3,1,16,512]{3,2,1,0:T(8,128)S(1)}, f32[3,1,16,512]{3,2,1,0:T(8,128)S(1)}, u32[]{:S(2)}, u32[]{:S(2)}) collective-permute-start(f32[3,1,16,512]{3,2,1,0:T(8,128)S(1)} %get-tuple-element.58), channel_id=1, source_target_pairs={{0,4},{4,8},{8,12},{12,16},{16,20},{20,24},{24,28},{1,5},{5,9},{9,... | collective-permute-start | bytes 294920 | tf_op jit(solution)/shard_map/ppermute | solution.py:21
  223.5 6.8 %collective-permute-start.5 = (f32[3,1,16,512]{3,2,1,0:T(8,128)S(1)}, f32[3,1,16,512]{3,2,1,0:T(8,128)S(1)}, u32[]{:S(2)}, u32[]{:S(2)}) collective-permute-start(f32[3,1,16,512]{3,2,1,0:T(8,128)S(1)} %get-tuple-element.57), channel_id=1, source_target_pairs={{4,0},{8,4},{12,8},{16,12},{20,16},{24,20},{28,24},{5,1},{9,5},{13... | collective-permute-start | bytes 294920 | tf_op jit(solution)/shard_map/ppermute | solution.py:23
  230.5 5.9 %collective-permute-start.6 = (f32[3,18,1,512]{3,2,1,0:T(1,128)S(1)}, f32[3,18,1,512]{3,2,1,0:T(1,128)S(1)}, u32[]{:S(2)}, u32[]{:S(2)}) collective-permute-start(f32[3,18,1,512]{3,2,1,0:T(1,128)S(1)} %get-tuple-element.51), channel_id=1, source_target_pairs={{0,1},{1,2},{2,3},{4,5},{5,6},{6,7},{8,9},{9,10},{10,11},{12,13},{... | collective-permute-start | bytes 331784 | tf_op jit(solution)/shard_map/ppermute | solution.py:21
  234.3 5.5 %collective-permute-start.7 = (f32[3,18,1,512]{3,2,1,0:T(1,128)S(1)}, f32[3,18,1,512]{3,2,1,0:T(1,128)S(1)}, u32[]{:S(2)}, u32[]{:S(2)}) collective-permute-start(f32[3,18,1,512]{3,2,1,0:T(1,128)S(1)} %get-tuple-element.52), channel_id=1, source_target_pairs={{1,0},{2,1},{3,2},{5,4},{6,5},{7,6},{9,8},{10,9},{11,10},{13,12},{... | collective-permute-start | bytes 331784 | tf_op jit(solution)/shard_map/ppermute | solution.py:23
  241.6 1.9 copy-start.3
  253.2 11.2 %copy-start.1 = (f32[6,16,16,512]{3,2,1,0:T(8,128)}, f32[6,16,16,512]{3,2,1,0:T(8,128)S(1)}, u32[]{:S(2)}) copy-start(f32[6,16,16,512]{3,2,1,0:T(8,128)S(1)} %get-tuple-element.6) | copy-start | bytes 9437188
  253.2 5.8 %collective-permute-start.8 = (f32[6,1,16,512]{3,2,1,0:T(8,128)S(1)}, f32[6,1,16,512]{3,2,1,0:T(8,128)S(1)}, u32[]{:S(2)}, u32[]{:S(2)}) collective-permute-start(f32[6,1,16,512]{3,2,1,0:T(8,128)S(1)} %get-tuple-element.45), channel_id=1, source_target_pairs={{0,4},{4,8},{8,12},{12,16},{16,20},{20,24},{24,28},{1,5},{5,9},{9,... | collective-permute-start | bytes 589832 | tf_op jit(solution)/shard_map/ppermute | solution.py:21
  256.5 7.9 %collective-permute-start.9 = (f32[6,1,16,512]{3,2,1,0:T(8,128)S(1)}, f32[6,1,16,512]{3,2,1,0:T(8,128)S(1)}, u32[]{:S(2)}, u32[]{:S(2)}) collective-permute-start(f32[6,1,16,512]{3,2,1,0:T(8,128)S(1)} %get-tuple-element.46), channel_id=1, source_target_pairs={{4,0},{8,4},{12,8},{16,12},{20,16},{24,20},{28,24},{5,1},{9,5},{13... | collective-permute-start | bytes 589832 | tf_op jit(solution)/shard_map/ppermute | solution.py:23
  264.4 7.4 %copy-start.25 = (f32[6,1,16,512]{3,2,1,0:T(8,128)}, f32[6,1,16,512]{3,2,1,0:T(8,128)S(1)}, u32[]{:S(2)}) copy-start(f32[6,1,16,512]{3,2,1,0:T(8,128)S(1)} %collective-permute-done.9) | copy-start | bytes 589828
  265.6 11.7 %collective-permute-start.10 = (f32[6,18,1,512]{3,2,1,0:T(1,128)}, f32[6,18,1,512]{3,2,1,0:T(1,128)}, u32[]{:S(2)}, u32[]{:S(2)}) collective-permute-start(f32[6,18,1,512]{3,2,1,0:T(1,128)} %get-tuple-element.30), channel_id=1, source_target_pairs={{0,1},{1,2},{2,3},{4,5},{5,6},{6,7},{8,9},{9,10},{10,11},{12,13},{... | collective-permute-start | bytes 663560 | tf_op jit(solution)/shard_map/ppermute | solution.py:21
  267.5 9.8 %collective-permute-start.11 = (f32[6,18,1,512]{3,2,1,0:T(1,128)}, f32[6,18,1,512]{3,2,1,0:T(1,128)}, u32[]{:S(2)}, u32[]{:S(2)}) collective-permute-start(f32[6,18,1,512]{3,2,1,0:T(1,128)} %get-tuple-element.31), channel_id=1, source_target_pairs={{1,0},{2,1},{3,2},{5,4},{6,5},{7,6},{9,8},{10,9},{11,10},{13,12},{... | collective-permute-start | bytes 663560 | tf_op jit(solution)/shard_map/ppermute | solution.py:23
  273.4 3.9 copy-start.2
  283.1 1.8 copy-start.5
  283.1 1.8 copy-start.13
  291.8 5.3 %copy-start.10 = (f32[16,16,512]{2,1,0:T(8,128)S(1)}, f32[16,16,512]{2,1,0:T(8,128)}, u32[]{:S(2)}) copy-start(f32[16,16,512]{2,1,0:T(8,128)} %fusion.25) | copy-start | bytes 1572868
  328.6 2.9 copy-start.12
  331.5 12.5 %copy-start.9 = (f32[8192,16]{0,1:T(8,128)S(1)}, f32[8192,16]{0,1:T(8,128)}, u32[]{:S(2)}) copy-start(f32[8192,16]{0,1:T(8,128)} %copy-done.8) | copy-start | bytes 1572868
  331.5 12.5 %copy-start.14 = (f32[2,8,16,512]{3,1,2,0:T(8,128)S(1)}, f32[2,8,16,512]{3,1,2,0:T(8,128)}, u32[]{:S(2)}) copy-start(f32[2,8,16,512]{3,1,2,0:T(8,128)} %copy.72) | copy-start | bytes 1572868
  331.5 13.4 %copy-start.16 = (f32[1,16,16,512]{3,2,1,0:T(8,128)S(1)}, f32[1,16,16,512]{3,2,1,0:T(8,128)}, u32[]{:S(2)}) copy-start(f32[1,16,16,512]{3,2,1,0:T(8,128)} %get-tuple-element.54) | copy-start | bytes 1572868
  462.5 10.7 %copy-start.6 = (f32[3,16,16,512]{3,2,1,0:T(8,128)}, f32[3,16,16,512]{3,2,1,0:T(8,128)S(1)}, u32[]{:S(2)}) copy-start(f32[3,16,16,512]{3,2,1,0:T(8,128)S(1)} %all_to_all.61) | copy-start | bytes 4718596
  462.5 5.5 %collective-permute-start.12 = (f32[3,1,16,512]{3,2,1,0:T(8,128)S(1)}, f32[3,1,16,512]{3,2,1,0:T(8,128)S(1)}, u32[]{:S(2)}, u32[]{:S(2)}) collective-permute-start(f32[3,1,16,512]{3,2,1,0:T(8,128)S(1)} %get-tuple-element.56), channel_id=1, source_target_pairs={{0,4},{4,8},{8,12},{12,16},{16,20},{20,24},{24,28},{1,5},{5,9},{9,... | collective-permute-start | bytes 294920 | tf_op jit(solution)/shard_map/ppermute | solution.py:21
  466.1 6.8 %collective-permute-start.13 = (f32[3,1,16,512]{3,2,1,0:T(8,128)S(1)}, f32[3,1,16,512]{3,2,1,0:T(8,128)S(1)}, u32[]{:S(2)}, u32[]{:S(2)}) collective-permute-start(f32[3,1,16,512]{3,2,1,0:T(8,128)S(1)} %get-tuple-element.55), channel_id=1, source_target_pairs={{4,0},{8,4},{12,8},{16,12},{20,16},{24,20},{28,24},{5,1},{9,5},{13... | collective-permute-start | bytes 294920 | tf_op jit(solution)/shard_map/ppermute | solution.py:23
  473.1 5.9 %collective-permute-start.14 = (f32[3,18,1,512]{3,2,1,0:T(1,128)S(1)}, f32[3,18,1,512]{3,2,1,0:T(1,128)S(1)}, u32[]{:S(2)}, u32[]{:S(2)}) collective-permute-start(f32[3,18,1,512]{3,2,1,0:T(1,128)S(1)} %get-tuple-element.49), channel_id=1, source_target_pairs={{0,1},{1,2},{2,3},{4,5},{5,6},{6,7},{8,9},{9,10},{10,11},{12,13},{... | collective-permute-start | bytes 331784 | tf_op jit(solution)/shard_map/ppermute | solution.py:21
  476.9 5.5 %collective-permute-start.15 = (f32[3,18,1,512]{3,2,1,0:T(1,128)S(1)}, f32[3,18,1,512]{3,2,1,0:T(1,128)S(1)}, u32[]{:S(2)}, u32[]{:S(2)}) collective-permute-start(f32[3,18,1,512]{3,2,1,0:T(1,128)S(1)} %get-tuple-element.50), channel_id=1, source_target_pairs={{1,0},{2,1},{3,2},{5,4},{6,5},{7,6},{9,8},{10,9},{11,10},{13,12},{... | collective-permute-start | bytes 331784 | tf_op jit(solution)/shard_map/ppermute | solution.py:23
  488.4 1.0 copy-start.22
  489.0 1.1 copy-start.19
  490.8 1.7 copy-start.26
  (4 other events, 4.2 us)
Sparse Core Ops, SparseCore 0:
  40.7 43.2 all-gather.4
  286.8 41.7 all-gather.6
where the time goes:
time: 505 us; the launch traced here: 499 us
  local copies, waits for them, and re-layouts  145 us (29%)
  blocking collectives  120 us (24%)
  waiting for transfers between devices  86.1 us (17%)
  other arithmetic  70.9 us (14%)
  starting transfers between devices  45.2 us (9%)
  matrix products  17.4 us (3%)
  between operations  15.1 us (3%)
    unnamed x88, local copies, waits for them, and re-layouts  65.1 us
    all_gather x2, waiting for transfers between devices, body(): piece = lax.all_gather(velocity[2], 'gy', axis=1, tiled=True)  55.9 us
    all_to_all x2, blocking collectives, damp_columns(): lax.all_to_all(velocity, 'gx', split_axis=3, concat_axis=1, tiled=True)  52.6 us
    all_to_all x2, blocking collectives, damp_columns(): return lax.all_to_all(damped, 'gx', split_axis=1, concat_axis=3, tiled=True)  48.9 us
    ppermute x8, starting transfers between devices, extended(): lax.ppermute(tail, axis, [(i, (i + 1) % count) for i in range(ends)])  26.7 us
    ppermute x8, waiting for transfers between devices, extended(): lax.ppermute(head, axis, [((i + 1) % count, i) for i in range(ends)])  26.2 us
    all_gather x2, blocking collectives, body(): all_force = lax.all_gather(force, 'gy', axis=1, tiled=True)  18.4 us
    ppermute x8, starting transfers between devices, extended(): lax.ppermute(head, axis, [((i + 1) % count, i) for i in range(ends)])  18.2 us
  transfers between devices with their start and end apart: 18, of which 12 were waited for; matrix products, arithmetic and copies ran while one was open for 8% of the time, Pallas kernels for 0%

commit v1 on v0

--- a/solution.py
+++ b/solution.py
@@ -8,6 +8,17 @@
 grid_ratio = 0.25
 soil_gain = 0.2
 pier_gain = 0.5
+
+
+def cut_along(x, dim, peers):
+    before, after = (x.shape[:dim], x.shape[dim + 1 :])
+    return jnp.moveaxis(x.reshape(*before, peers, -1, *after), dim, 0)
+
+
+def in_order(pieces, dim):
+    pieces = jnp.moveaxis(pieces, 0, dim)
+    dims = pieces.shape
+    return pieces.reshape(*dims[:dim], dims[dim] * dims[dim + 1], *dims[dim + 2 :])
 
 
 def extended(cells, sides, width):
@@ -103,7 +114,15 @@
 
 
 def damp_columns(velocity, inverse):
-    pencils = lax.all_to_all(velocity, "gx", split_axis=3, concat_axis=1, tiled=True)
+    size, index = (lax.axis_size("gx"), lax.axis_index("gx"))
+    tiles = cut_along(velocity, 3, size)
+    whole = tiles
+    for hop in range(1, size):
+        target, source = ((index + hop) % size, (index - hop) % size)
+        sent = lax.dynamic_index_in_dim(tiles, target, 0)
+        other = lax.ppermute(sent, "gx", [(i_2, (i_2 + hop) % size) for i_2 in range(size)])
+        whole = lax.dynamic_update_slice_in_dim(whole, other, source, axis=0)
+    pencils = in_order(whole, 1)
     shape = pencils.shape
     flat = pencils.reshape(shape[0], shape[1], shape[2] * shape[3])
     damped = jnp.einsum("zk,fkm->fzm", inverse, flat, precision=lax.Precision.HIGHEST).reshape(

time: 505 us -> 482 us (0.954)
  waiting for transfers between devices: 86.1 us -> 145 us
  blocking collectives: 120 us -> 63.9 us
  local copies, waits for them, and re-layouts: 145 us -> 97.5 us
  starting transfers between devices: 45.2 us -> 77.2 us
  other arithmetic: 70.9 us -> 57.3 us
    ppermute x0 -> x14, waiting for transfers between devices: none -> 60.5 us  [damp_columns(): lax.ppermute(sent, 'gx', [(i_2, (i_2 + hop) % size) for i_2 in range(size)])]
    all_to_all x2 -> x0, blocking collectives: 52.6 us -> none  [damp_columns(): lax.all_to_all(velocity, 'gx', split_axis=3, concat_axis=1, tiled=True)]
    ppermute x0 -> x14, starting transfers between devices: none -> 31.2 us  [damp_columns(): lax.ppermute(sent, 'gx', [(i_2, (i_2 + hop) % size) for i_2 in range(size)])]
    unnamed x88 -> x82, local copies, waits for them, and re-layouts: 65.1 us -> 34.9 us
    all_to_all x3 -> x0, local copies, waits for them, and re-layouts: 16.8 us -> none  [damp_columns(): lax.all_to_all(velocity, 'gx', split_axis=3, concat_axis=1, tiled=True)]
    another operation x4 -> x0, other arithmetic: 11.1 us -> none  [the longest x2 10.7 us: move_velocity(): return jnp.stack([first, second, third])]
    all_to_all x2 -> x0, other arithmetic: 8.82 us -> none  [damp_columns(): lax.all_to_all(velocity, 'gx', split_axis=3, concat_axis=1, tiled=True)]
    another operation x2 -> x8, local copies, waits for them, and re-layouts: 17.6 us -> 13.4 us  [body(): jnp.stack([velocity[0], velocity[1], vertical.reshape(depth_cells, side_c...]
  transfers between devices with their start and end apart: 18 -> 32, of which waited for: 12 -> 19; matrix products, arithmetic and copies ran while one was open for 8% -> 10% of each run, Pallas kernels for 0% -> 0%
where the time goes in v1:
time: 482 us; the launch traced here: 475 us
  waiting for transfers between devices  145 us (30%)
  local copies, waits for them, and re-layouts  97.5 us (20%)
  starting transfers between devices  77.2 us (16%)
  blocking collectives  63.9 us (13%)
  other arithmetic  57.3 us (12%)
  matrix products  19 us (4%)
  between operations  15.3 us (3%)
    ppermute x14, waiting for transfers between devices, damp_columns(): lax.ppermute(sent, 'gx', [(i_2, (i_2 + hop) % size) for i_2 in range(size)])  60.5 us
    all_gather x2, waiting for transfers between devices, body(): piece = lax.all_gather(velocity[2], 'gy', axis=1, tiled=True)  54.3 us
    all_to_all x2, blocking collectives, damp_columns(): return lax.all_to_all(damped, 'gx', split_axis=1, concat_axis=3, tiled=True)  45.4 us
    unnamed x82, local copies, waits for them, and re-layouts  34.9 us
    ppermute x14, starting transfers between devices, damp_columns(): lax.ppermute(sent, 'gx', [(i_2, (i_2 + hop) % size) for i_2 in range(size)])  31.2 us
    ppermute x8, starting transfers between devices, extended(): lax.ppermute(tail, axis, [(i, (i + 1) % count) for i in range(ends)])  27.1 us
    ppermute x8, waiting for transfers between devices, extended(): lax.ppermute(head, axis, [((i + 1) % count, i) for i in range(ends)])  25.5 us
    all_gather x2, blocking collectives, body(): all_force = lax.all_gather(force, 'gy', axis=1, tiled=True)  18.6 us
  transfers between devices with their start and end apart: 32, of which 19 were waited for; matrix products, arithmetic and copies ran while one was open for 10% of the time, Pallas kernels for 0%

profile of v1, /device:TPU:11, one launch (start us, length us, event | category | flops | bytes accessed | tf_op | source)
XLA Modules:
  0.0 475.2 jit_solution(10627007882308053709)
XLA Ops:
  8.3 3.7 collective-permute-start
  16.9 3.0 collective-permute-done.1
  20.3 3.2 collective-permute-start.2
  25.6 2.9 collective-permute-done.2
  28.5 3.2 collective-permute-done.3
  31.7 4.2 select_maximum_fusion.4
  40.9 2.9 convert_reduce_fusion.1
  56.4 27.4 %all-gather.5.cloned.1.call-done = f32[16,64,512]{2,1,0:T(8,128)} async-done(((f32[16,16,512]{2,1,0:T(8,128)}), f32[16,64,512]{2,1,0:T(8,128)}) %all-gather.5.cloned.1.call-update) | async-done | bytes 2097168 | tf_op jit(solution)/shard_map/all_gather | solution.py:160
  83.7 2.9 copy.82
  89.3 9.2 %all-gather = f32[4,4,16]{2,1,0:T(4,128)S(1)} all-gather(f32[1,4,16]{2,1,0:T(4,128)S(1)} %bitcast.218), channel_id=1, replica_groups=mesh['gx'=8,'gy'=4] {'gy'}, dimensions={0}, use_global_device_ids=true | all-gather | bytes 1280 | tf_op jit(solution)/shard_map/all_gather | solution.py:171
  105.3 4.1 collective-permute-start.4
  113.0 5.3 %collective-permute-done.4 = f32[1,3,16,16,64]{4,3,2,0,1:T(8,128)} collective-permute-done((f32[1,3,16,16,64]{4,3,2,0,1:T(8,128)}, f32[1,3,16,16,64]{4,3,2,0,1:T(8,128)}, u32[]{:S(2)}, u32[]{:S(2)}) %collective-permute-start.4) | collective-permute-done | bytes 196640 | tf_op jit(solution)/shard_map/ppermute | solution.py:123
  118.2 11.9 %collective-permute-start.6 = (f32[1,3,16,16,64]{4,3,2,0,1:T(8,128)}, f32[1,3,16,16,64]{4,3,2,0,1:T(8,128)S(1)}, u32[]{:S(2)}, u32[]{:S(2)}) collective-permute-start(f32[1,3,16,16,64]{4,3,2,0,1:T(8,128)} %get-tuple-element.58), channel_id=1, source_target_pairs={{0,12},{4,16},{8,20},{12,24},{16,28},{20,0},{24,4},{28,8},{1,13},{... | collective-permute-start | bytes 589832 | tf_op jit(solution)/shard_map/ppermute | solution.py:123
  132.5 15.6 %collective-permute-done.6 = f32[1,3,16,16,64]{4,3,2,0,1:T(8,128)S(1)} collective-permute-done((f32[1,3,16,16,64]{4,3,2,0,1:T(8,128)}, f32[1,3,16,16,64]{4,3,2,0,1:T(8,128)S(1)}, u32[]{:S(2)}, u32[]{:S(2)}) %collective-permute-start.6) | collective-permute-done | bytes 196640 | tf_op jit(solution)/shard_map/ppermute | solution.py:123
  148.1 5.8 %collective-permute-done.7 = f32[1,3,16,16,64]{4,3,2,0,1:T(8,128)S(1)} collective-permute-done((f32[1,3,16,16,64]{4,3,2,0,1:T(8,128)}, f32[1,3,16,16,64]{4,3,2,0,1:T(8,128)S(1)}, u32[]{:S(2)}, u32[]{:S(2)}) %collective-permute-start.7) | collective-permute-done | bytes 196640 | tf_op jit(solution)/shard_map/ppermute | solution.py:123
  155.9 5.2 %fusion.61 = f32[3,1024,128]{2,1,0:T(8,128)} fusion(f32[3,128,1024]{2,1,0:T(8,128)} %reshape_reshape.6, f32[128,128]{1,0:T(8,128)S(1)} %copy-done), kind=kOutput, calls=%fused_computation.174 | convolution fusion | flops 603979776 | bytes 3211264 | tf_op jit(solution)/shard_map/zk,fkm->fzm/dot_general | solution.py:128
  163.4 3.0 reshape.107
  166.4 22.3 %all_to_all.36 = f32[8,1,49152]{2,1,0:T(1,128)S(1)} all-to-all(f32[8,1,49152]{2,1,0:T(1,128)} %reshape.107), channel_id=1, replica_groups=mesh['gx'=8,'gy'=4] {'gx'}, dimensions={0} | all-to-all | bytes 3145728 | tf_op jit(solution)/shard_map/all_to_all | solution.py:131
  189.3 6.1 %reduce = f32[8,49152]{1,0:T(8,128)} reduce(f32[8,1,49152]{2,1,0:T(1,128)S(1)} %all_to_all.36, f32[]{:T(128)} %broadcast.172), dimensions={1}, to_apply=%all_to_all.26.reduce_sub_computation | reduce | bytes 3145732 | tf_op jit(solution)/shard_map/all_to_all | solution.py:131
  198.1 3.5 copy.67
  201.6 3.8 all_to_all.29
  206.3 4.0 collective-permute-start.11
  214.0 3.3 collective-permute-done.12
  217.6 3.8 collective-permute-start.13
  223.5 3.3 collective-permute-done.14
  240.3 3.2 collective-permute-start.15
  246.8 4.7 collective-permute-done.16
  254.6 4.4 collective-permute-start.18
  270.0 5.8 %select_maximum_fusion = f32[6,18,18,514]{3,2,1,0:T(8,128)S(1)} fusion(f32[6,18,1,512]{3,2,1,0:T(1,128)} %collective-permute-done.18, f32[6,18,1,512]{3,2,1,0:T(1,128)} %collective-permute-done.17, f32[6,1,16,512]{3,2,1,0:T(8,128)} %copy-done.23, f32[6,16,16,512]{3,2,1,0:T(8,128)S(1)} %copy-done.2, f32[6,1,16,512]{3,2,1,0:T(8,128)S(1)} %collective-permute-done.15), kind=kLoop, calls=%fused_computation.9 | loop fusion | flops 11990592 | bytes 7978176 | tf_op jit(solution)/shard_map/concatenate | solution.py:30
  279.9 2.9 copy.68
  294.8 26.9 %all-gather.7.cloned.1.call-done = f32[16,64,512]{2,1,0:T(8,128)} async-done(((f32[16,16,512]{2,1,0:T(8,128)}), f32[16,64,512]{2,1,0:T(8,128)}) %all-gather.7.cloned.1.call-update) | async-done | bytes 2097168 | tf_op jit(solution)/shard_map/all_gather | solution.py:160
  321.7 2.9 copy.84
  324.7 3.2 multiply_subtract_fusion
  327.9 9.4 %all-gather.1 = f32[4,4,16]{2,1,0:T(4,128)S(1)} all-gather(f32[1,4,16]{2,1,0:T(4,128)S(1)} %bitcast.219), channel_id=1, replica_groups=mesh['gx'=8,'gy'=4] {'gy'}, dimensions={0}, use_global_device_ids=true | all-gather | bytes 1280 | tf_op jit(solution)/shard_map/all_gather | solution.py:171
  342.9 4.2 collective-permute-start.19
  350.5 4.9 %collective-permute-done.19 = f32[1,3,16,16,64]{4,3,2,0,1:T(8,128)S(1)} collective-permute-done((f32[1,3,16,16,64]{4,3,2,0,1:T(8,128)S(1)}, f32[1,3,16,16,64]{4,3,2,0,1:T(8,128)S(1)}, u32[]{:S(2)}, u32[]{:S(2)}) %collective-permute-start.19) | collective-permute-done | bytes 196640 | tf_op jit(solution)/shard_map/ppermute | solution.py:123
  357.9 6.9 %collective-permute-done.20 = f32[1,3,16,16,64]{4,3,2,0,1:T(8,128)S(1)} collective-permute-done((f32[1,3,16,16,64]{4,3,2,0,1:T(8,128)S(1)}, f32[1,3,16,16,64]{4,3,2,0,1:T(8,128)S(1)}, u32[]{:S(2)}, u32[]{:S(2)}) %collective-permute-start.20) | collective-permute-done | bytes 196640 | tf_op jit(solution)/shard_map/ppermute | solution.py:123
  366.0 16.3 %collective-permute-done.21 = f32[1,3,16,16,64]{4,3,2,0,1:T(8,128)S(1)} collective-permute-done((f32[1,3,16,16,64]{4,3,2,0,1:T(8,128)S(1)}, f32[1,3,16,16,64]{4,3,2,0,1:T(8,128)S(1)}, u32[]{:S(2)}, u32[]{:S(2)}) %collective-permute-start.21) | collective-permute-done | bytes 196640 | tf_op jit(solution)/shard_map/ppermute | solution.py:123
  382.3 5.8 %collective-permute-done.22 = f32[1,3,16,16,64]{4,3,2,0,1:T(8,128)S(1)} collective-permute-done((f32[1,3,16,16,64]{4,3,2,0,1:T(8,128)S(1)}, f32[1,3,16,16,64]{4,3,2,0,1:T(8,128)S(1)}, u32[]{:S(2)}, u32[]{:S(2)}) %collective-permute-start.22) | collective-permute-done | bytes 196640 | tf_op jit(solution)/shard_map/ppermute | solution.py:123
  390.1 5.2 %fusion.59 = f32[3,1024,128]{2,1,0:T(8,128)} fusion(f32[3,128,1024]{2,1,0:T(8,128)} %reshape_reshape.7, f32[128,128]{1,0:T(8,128)S(1)} %copy-done), kind=kOutput, calls=%fused_computation.172 | convolution fusion | flops 603979776 | bytes 3211264 | tf_op jit(solution)/shard_map/zk,fkm->fzm/dot_general | solution.py:128
  397.6 3.0 reshape.109
  400.6 23.0 %all_to_all.37 = f32[8,1,49152]{2,1,0:T(1,128)S(1)} all-to-all(f32[8,1,49152]{2,1,0:T(1,128)} %reshape.109), channel_id=1, replica_groups=mesh['gx'=8,'gy'=4] {'gx'}, dimensions={0} | all-to-all | bytes 3145728 | tf_op jit(solution)/shard_map/all_to_all | solution.py:131
  423.6 6.1 %reduce.1 = f32[8,49152]{1,0:T(8,128)} reduce(f32[8,1,49152]{2,1,0:T(1,128)S(1)} %all_to_all.37, f32[]{:T(128)} %broadcast.172), dimensions={1}, to_apply=%all_to_all.30.reduce_sub_computation | reduce | bytes 3145732 | tf_op jit(solution)/shard_map/all_to_all | solution.py:131
  432.4 3.5 copy.76
  438.8 3.6 collective-permute-start.26
  444.5 4.7 collective-permute-done.27
  449.4 3.7 collective-permute-start.28
  455.3 3.3 collective-permute-done.29
  (194 shorter events, 138.8 us)
Async XLA Ops:
  7.2 148.8 %copy-start = (f32[128,128]{1,0:T(8,128)S(1)}, f32[128,128]{1,0:T(8,128)}, u32[]{:S(2)}) copy-start(f32[128,128]{1,0:T(8,128)} %param.21) | copy-start | bytes 196612
  7.2 76.5 %all-gather.5.cloned.1.call-start = ((), (), s32[]{:S(2)}) async-start(), calls=%async_computation.2 | async-start | bytes 2621440 | tf_op jit(solution)/shard_map/all_gather | solution.py:160
  8.3 6.3 %collective-permute-start = (f32[6,1,16,512]{3,2,1,0:T(8,128)S(1)}, f32[6,1,16,512]{3,2,1,0:T(8,128)S(1)}, u32[]{:S(2)}, u32[]{:S(2)}) collective-permute-start(f32[6,1,16,512]{3,2,1,0:T(8,128)S(1)} %get-tuple-element.62), channel_id=1, source_target_pairs={{0,4},{4,8},{8,12},{12,16},{16,20},{20,24},{24,28},{1,5},{5,9},{9,... | collective-permute-start | bytes 589832 | tf_op jit(solution)/shard_map/ppermute | solution.py:32
  12.0 7.9 %collective-permute-start.1 = (f32[6,1,16,512]{3,2,1,0:T(8,128)S(1)}, f32[6,1,16,512]{3,2,1,0:T(8,128)S(1)}, u32[]{:S(2)}, u32[]{:S(2)}) collective-permute-start(f32[6,1,16,512]{3,2,1,0:T(8,128)S(1)} %get-tuple-element.61), channel_id=1, source_target_pairs={{4,0},{8,4},{12,8},{16,12},{20,16},{24,20},{28,24},{5,1},{9,5},{13... | collective-permute-start | bytes 589832 | tf_op jit(solution)/shard_map/ppermute | solution.py:34
  20.3 8.2 %collective-permute-start.2 = (f32[6,18,1,512]{3,2,1,0:T(1,128)S(1)}, f32[6,18,1,512]{3,2,1,0:T(1,128)S(1)}, u32[]{:S(2)}, u32[]{:S(2)}) collective-permute-start(f32[6,18,1,512]{3,2,1,0:T(1,128)S(1)} %get-tuple-element.32), channel_id=1, source_target_pairs={{0,1},{1,2},{2,3},{4,5},{5,6},{6,7},{8,9},{9,10},{10,11},{12,13},{... | collective-permute-start | bytes 663560 | tf_op jit(solution)/shard_map/ppermute | solution.py:32
  23.5 8.2 %collective-permute-start.3 = (f32[6,18,1,512]{3,2,1,0:T(1,128)S(1)}, f32[6,18,1,512]{3,2,1,0:T(1,128)S(1)}, u32[]{:S(2)}, u32[]{:S(2)}) collective-permute-start(f32[6,18,1,512]{3,2,1,0:T(1,128)S(1)} %get-tuple-element.33), channel_id=1, source_target_pairs={{1,0},{2,1},{3,2},{5,4},{6,5},{7,6},{9,8},{10,9},{11,10},{13,12},{... | collective-permute-start | bytes 663560 | tf_op jit(solution)/shard_map/ppermute | solution.py:34
  40.3 281.4 %all-gather.7.cloned.1.call-start = ((), (), s32[]{:S(2)}) async-start(), calls=%async_computation.3 | async-start | bytes 2621440 | tf_op jit(solution)/shard_map/all_gather | solution.py:160
  54.9 31.7 %copy-start.26 = (f32[16,4]{0,1:T(4,128)S(1)}, f32[16,4]{0,1:T(4,128)}, u32[]{:S(2)}) copy-start(f32[16,4]{0,1:T(4,128)} %param.13) | copy-start | bytes 772
  54.9 31.7 %copy-start.27 = (f32[4]{0:T(128)S(1)}, f32[4]{0:T(128)}, u32[]{:S(2)}) copy-start(f32[4]{0:T(128)} %param.19) | copy-start | bytes 52
  83.7 14.8 %copy-start.7 = (f32[8192,16]{0,1:T(8,128)S(1)}, f32[8192,16]{0,1:T(8,128)}, u32[]{:S(2)}) copy-start(f32[8192,16]{0,1:T(8,128)} %convert_reduce_fusion) | copy-start | bytes 1572868
  83.7 14.8 %copy-start.15 = (f32[2,8,16,512]{3,1,2,0:T(8,128)S(1)}, f32[2,8,16,512]{3,1,2,0:T(8,128)}, u32[]{:S(2)}) copy-start(f32[2,8,16,512]{3,1,2,0:T(8,128)} %copy.81) | copy-start | bytes 1572868
  105.3 12.9 %collective-permute-start.4 = (f32[1,3,16,16,64]{4,3,2,0,1:T(8,128)}, f32[1,3,16,16,64]{4,3,2,0,1:T(8,128)}, u32[]{:S(2)}, u32[]{:S(2)}) collective-permute-start(f32[1,3,16,16,64]{4,3,2,0,1:T(8,128)} %get-tuple-element.60), channel_id=1, source_target_pairs={{0,4},{4,8},{8,12},{12,16},{16,20},{20,24},{24,28},{28,0},{1,5},{5... | collective-permute-start | bytes 589832 | tf_op jit(solution)/shard_map/ppermute | solution.py:123
  109.5 21.7 %collective-permute-start.5 = (f32[1,3,16,16,64]{4,3,2,0,1:T(8,128)}, f32[1,3,16,16,64]{4,3,2,0,1:T(8,128)}, u32[]{:S(2)}, u32[]{:S(2)}) collective-permute-start(f32[1,3,16,16,64]{4,3,2,0,1:T(8,128)} %get-tuple-element.59), channel_id=1, source_target_pairs={{0,8},{4,12},{8,16},{12,20},{16,24},{20,28},{24,0},{28,4},{1,9},{5... | collective-permute-start | bytes 589832 | tf_op jit(solution)/shard_map/ppermute | solution.py:123
  110.7 43.4 %collective-permute-start.10 = (f32[1,3,16,16,64]{4,3,2,0,1:T(8,128)}, f32[1,3,16,16,64]{4,3,2,0,1:T(8,128)S(1)}, u32[]{:S(2)}, u32[]{:S(2)}) collective-permute-start(f32[1,3,16,16,64]{4,3,2,0,1:T(8,128)} %get-tuple-element.54), channel_id=1, source_target_pairs={{0,28},{4,0},{8,4},{12,8},{16,12},{20,16},{24,20},{28,24},{1,29},{... | collective-permute-start | bytes 589832 | tf_op jit(solution)/shard_map/ppermute | solution.py:123
  110.7 43.4 %collective-permute-start.9 = (f32[1,3,16,16,64]{4,3,2,0,1:T(8,128)}, f32[1,3,16,16,64]{4,3,2,0,1:T(8,128)S(1)}, u32[]{:S(2)}, u32[]{:S(2)}) collective-permute-start(f32[1,3,16,16,64]{4,3,2,0,1:T(8,128)} %get-tuple-element.55), channel_id=1, source_target_pairs={{0,24},{4,28},{8,0},{12,4},{16,8},{20,12},{24,16},{28,20},{1,25},{... | collective-permute-start | bytes 589832 | tf_op jit(solution)/shard_map/ppermute | solution.py:123
  111.0 43.0 %collective-permute-start.8 = (f32[1,3,16,16,64]{4,3,2,0,1:T(8,128)}, f32[1,3,16,16,64]{4,3,2,0,1:T(8,128)S(1)}, u32[]{:S(2)}, u32[]{:S(2)}) collective-permute-start(f32[1,3,16,16,64]{4,3,2,0,1:T(8,128)} %get-tuple-element.56), channel_id=1, source_target_pairs={{0,20},{4,24},{8,28},{12,0},{16,4},{20,8},{24,12},{28,16},{1,21},{... | collective-permute-start | bytes 589832 | tf_op jit(solution)/shard_map/ppermute | solution.py:123
  118.2 29.9 %collective-permute-start.6 = (f32[1,3,16,16,64]{4,3,2,0,1:T(8,128)}, f32[1,3,16,16,64]{4,3,2,0,1:T(8,128)S(1)}, u32[]{:S(2)}, u32[]{:S(2)}) collective-permute-start(f32[1,3,16,16,64]{4,3,2,0,1:T(8,128)} %get-tuple-element.58), channel_id=1, source_target_pairs={{0,12},{4,16},{8,20},{12,24},{16,28},{20,0},{24,4},{28,8},{1,13},{... | collective-permute-start | bytes 589832 | tf_op jit(solution)/shard_map/ppermute | solution.py:123
  131.2 22.8 %collective-permute-start.7 = (f32[1,3,16,16,64]{4,3,2,0,1:T(8,128)}, f32[1,3,16,16,64]{4,3,2,0,1:T(8,128)S(1)}, u32[]{:S(2)}, u32[]{:S(2)}) collective-permute-start(f32[1,3,16,16,64]{4,3,2,0,1:T(8,128)} %get-tuple-element.57), channel_id=1, source_target_pairs={{0,16},{4,20},{8,24},{12,28},{16,0},{20,4},{24,8},{28,12},{1,17},{... | collective-permute-start | bytes 589832 | tf_op jit(solution)/shard_map/ppermute | solution.py:123
  201.6 8.8 %copy-start.28 = (f32[8]{0:T(128)S(1)}, f32[8]{0:T(128)}, u32[]{:S(2)}) copy-start(f32[8]{0:T(128)} %param.18) | copy-start | bytes 100
  201.6 8.8 %copy-start.29 = (s32[16]{0:T(128)S(1)}, s32[16]{0:T(128)}, u32[]{:S(2)}) copy-start(s32[16]{0:T(128)} %param.15) | copy-start | bytes 196
  201.6 8.8 %copy-start.30 = (f32[8]{0:T(128)S(1)}, f32[8]{0:T(128)}, u32[]{:S(2)}) copy-start(f32[8]{0:T(128)} %param.17) | copy-start | bytes 100
  201.6 8.8 %copy-start.31 = (f32[8]{0:T(128)S(1)}, f32[8]{0:T(128)}, u32[]{:S(2)}) copy-start(f32[8]{0:T(128)} %param.16) | copy-start | bytes 100
  206.3 6.1 %collective-permute-start.11 = (f32[3,1,16,512]{3,2,1,0:T(8,128)S(1)}, f32[3,1,16,512]{3,2,1,0:T(8,128)S(1)}, u32[]{:S(2)}, u32[]{:S(2)}) collective-permute-start(f32[3,1,16,512]{3,2,1,0:T(8,128)S(1)} %get-tuple-element.72), channel_id=1, source_target_pairs={{0,4},{4,8},{8,12},{12,16},{16,20},{20,24},{24,28},{1,5},{5,9},{9,... | collective-permute-start | bytes 294920 | tf_op jit(solution)/shard_map/ppermute | solution.py:32
  210.5 6.8 %collective-permute-start.12 = (f32[3,1,16,512]{3,2,1,0:T(8,128)S(1)}, f32[3,1,16,512]{3,2,1,0:T(8,128)S(1)}, u32[]{:S(2)}, u32[]{:S(2)}) collective-permute-start(f32[3,1,16,512]{3,2,1,0:T(8,128)S(1)} %get-tuple-element.71), channel_id=1, source_target_pairs={{4,0},{8,4},{12,8},{16,12},{20,16},{24,20},{28,24},{5,1},{9,5},{13... | collective-permute-start | bytes 294920 | tf_op jit(solution)/shard_map/ppermute | solution.py:34
  217.6 5.9 %collective-permute-start.13 = (f32[3,18,1,512]{3,2,1,0:T(1,128)S(1)}, f32[3,18,1,512]{3,2,1,0:T(1,128)S(1)}, u32[]{:S(2)}, u32[]{:S(2)}) collective-permute-start(f32[3,18,1,512]{3,2,1,0:T(1,128)S(1)} %get-tuple-element.65), channel_id=1, source_target_pairs={{0,1},{1,2},{2,3},{4,5},{5,6},{6,7},{8,9},{9,10},{10,11},{12,13},{... | collective-permute-start | bytes 331784 | tf_op jit(solution)/shard_map/ppermute | solution.py:32
  221.3 5.5 %collective-permute-start.14 = (f32[3,18,1,512]{3,2,1,0:T(1,128)S(1)}, f32[3,18,1,512]{3,2,1,0:T(1,128)S(1)}, u32[]{:S(2)}, u32[]{:S(2)}) collective-permute-start(f32[3,18,1,512]{3,2,1,0:T(1,128)S(1)} %get-tuple-element.66), channel_id=1, source_target_pairs={{1,0},{2,1},{3,2},{5,4},{6,5},{7,6},{9,8},{10,9},{11,10},{13,12},{... | collective-permute-start | bytes 331784 | tf_op jit(solution)/shard_map/ppermute | solution.py:34
  240.3 11.2 %copy-start.1 = (f32[6,16,16,512]{3,2,1,0:T(8,128)}, f32[6,16,16,512]{3,2,1,0:T(8,128)S(1)}, u32[]{:S(2)}) copy-start(f32[6,16,16,512]{3,2,1,0:T(8,128)S(1)} %get-tuple-element.6) | copy-start | bytes 9437188
  240.3 6.5 %collective-permute-start.15 = (f32[6,1,16,512]{3,2,1,0:T(8,128)S(1)}, f32[6,1,16,512]{3,2,1,0:T(8,128)S(1)}, u32[]{:S(2)}, u32[]{:S(2)}) collective-permute-start(f32[6,1,16,512]{3,2,1,0:T(8,128)S(1)} %get-tuple-element.52), channel_id=1, source_target_pairs={{0,4},{4,8},{8,12},{12,16},{16,20},{20,24},{24,28},{1,5},{5,9},{9,... | collective-permute-start | bytes 589832 | tf_op jit(solution)/shard_map/ppermute | solution.py:32
  243.6 7.9 %collective-permute-start.16 = (f32[6,1,16,512]{3,2,1,0:T(8,128)S(1)}, f32[6,1,16,512]{3,2,1,0:T(8,128)S(1)}, u32[]{:S(2)}, u32[]{:S(2)}) collective-permute-start(f32[6,1,16,512]{3,2,1,0:T(8,128)S(1)} %get-tuple-element.53), channel_id=1, source_target_pairs={{4,0},{8,4},{12,8},{16,12},{20,16},{24,20},{28,24},{5,1},{9,5},{13... | collective-permute-start | bytes 589832 | tf_op jit(solution)/shard_map/ppermute | solution.py:34
  251.5 9.3 %copy-start.23 = (f32[6,1,16,512]{3,2,1,0:T(8,128)}, f32[6,1,16,512]{3,2,1,0:T(8,128)S(1)}, u32[]{:S(2)}) copy-start(f32[6,1,16,512]{3,2,1,0:T(8,128)S(1)} %collective-permute-done.16) | copy-start | bytes 589828
  252.7 17.3 %collective-permute-start.17 = (f32[6,18,1,512]{3,2,1,0:T(1,128)}, f32[6,18,1,512]{3,2,1,0:T(1,128)}, u32[]{:S(2)}, u32[]{:S(2)}) collective-permute-start(f32[6,18,1,512]{3,2,1,0:T(1,128)} %get-tuple-element.30), channel_id=1, source_target_pairs={{0,1},{1,2},{2,3},{4,5},{5,6},{6,7},{8,9},{9,10},{10,11},{12,13},{... | collective-permute-start | bytes 663560 | tf_op jit(solution)/shard_map/ppermute | solution.py:32
  254.6 15.3 %collective-permute-start.18 = (f32[6,18,1,512]{3,2,1,0:T(1,128)}, f32[6,18,1,512]{3,2,1,0:T(1,128)}, u32[]{:S(2)}, u32[]{:S(2)}) collective-permute-start(f32[6,18,1,512]{3,2,1,0:T(1,128)} %get-tuple-element.31), channel_id=1, source_target_pairs={{1,0},{2,1},{3,2},{5,4},{6,5},{7,6},{9,8},{10,9},{11,10},{13,12},{... | collective-permute-start | bytes 663560 | tf_op jit(solution)/shard_map/ppermute | solution.py:34
  262.4 7.6 %copy-start.2 = (f32[6,16,16,512]{3,2,1,0:T(8,128)S(1)}, f32[6,16,16,512]{3,2,1,0:T(8,128)}, u32[]{:S(2)}) copy-start(f32[6,16,16,512]{3,2,1,0:T(8,128)} %copy-done.1) | copy-start | bytes 9437188
  279.8 5.2 %copy-start.9 = (f32[16,16,512]{2,1,0:T(8,128)S(1)}, f32[16,16,512]{2,1,0:T(8,128)}, u32[]{:S(2)}) copy-start(f32[16,16,512]{2,1,0:T(8,128)} %get-tuple-element.67) | copy-start | bytes 1572868
  321.7 15.6 %copy-start.8 = (f32[8192,16]{0,1:T(8,128)S(1)}, f32[8192,16]{0,1:T(8,128)}, u32[]{:S(2)}) copy-start(f32[8192,16]{0,1:T(8,128)} %convert_reduce_fusion) | copy-start | bytes 1572868
  321.7 15.6 %copy-start.14 = (f32[2,8,16,512]{3,1,2,0:T(8,128)S(1)}, f32[2,8,16,512]{3,1,2,0:T(8,128)}, u32[]{:S(2)}) copy-start(f32[2,8,16,512]{3,1,2,0:T(8,128)} %copy.83) | copy-start | bytes 1572868
  342.9 12.6 %collective-permute-start.19 = (f32[1,3,16,16,64]{4,3,2,0,1:T(8,128)S(1)}, f32[1,3,16,16,64]{4,3,2,0,1:T(8,128)S(1)}, u32[]{:S(2)}, u32[]{:S(2)}) collective-permute-start(f32[1,3,16,16,64]{4,3,2,0,1:T(8,128)S(1)} %get-tuple-element.48), channel_id=1, source_target_pairs={{0,4},{4,8},{8,12},{12,16},{16,20},{20,24},{24,28},{28,0},{1,5},{5... | collective-permute-start | bytes 589832 | tf_op jit(solution)/shard_map/ppermute | solution.py:123
  347.0 17.8 %collective-permute-start.20 = (f32[1,3,16,16,64]{4,3,2,0,1:T(8,128)S(1)}, f32[1,3,16,16,64]{4,3,2,0,1:T(8,128)S(1)}, u32[]{:S(2)}, u32[]{:S(2)}) collective-permute-start(f32[1,3,16,16,64]{4,3,2,0,1:T(8,128)S(1)} %get-tuple-element.47), channel_id=1, source_target_pairs={{0,8},{4,12},{8,16},{12,20},{16,24},{20,28},{24,0},{28,4},{1,9},{5... | collective-permute-start | bytes 589832 | tf_op jit(solution)/shard_map/ppermute | solution.py:123
  348.2 40.0 %collective-permute-start.25 = (f32[1,3,16,16,64]{4,3,2,0,1:T(8,128)S(1)}, f32[1,3,16,16,64]{4,3,2,0,1:T(8,128)S(1)}, u32[]{:S(2)}, u32[]{:S(2)}) collective-permute-start(f32[1,3,16,16,64]{4,3,2,0,1:T(8,128)S(1)} %get-tuple-element.42), channel_id=1, source_target_pairs={{0,28},{4,0},{8,4},{12,8},{16,12},{20,16},{24,20},{28,24},{1,29},{... | collective-permute-start | bytes 589832 | tf_op jit(solution)/shard_map/ppermute | solution.py:123
  348.2 40.0 %collective-permute-start.24 = (f32[1,3,16,16,64]{4,3,2,0,1:T(8,128)S(1)}, f32[1,3,16,16,64]{4,3,2,0,1:T(8,128)S(1)}, u32[]{:S(2)}, u32[]{:S(2)}) collective-permute-start(f32[1,3,16,16,64]{4,3,2,0,1:T(8,128)S(1)} %get-tuple-element.43), channel_id=1, source_target_pairs={{0,24},{4,28},{8,0},{12,4},{16,8},{20,12},{24,16},{28,20},{1,25},{... | collective-permute-start | bytes 589832 | tf_op jit(solution)/shard_map/ppermute | solution.py:123
  348.5 39.6 %collective-permute-start.23 = (f32[1,3,16,16,64]{4,3,2,0,1:T(8,128)S(1)}, f32[1,3,16,16,64]{4,3,2,0,1:T(8,128)S(1)}, u32[]{:S(2)}, u32[]{:S(2)}) collective-permute-start(f32[1,3,16,16,64]{4,3,2,0,1:T(8,128)S(1)} %get-tuple-element.44), channel_id=1, source_target_pairs={{0,20},{4,24},{8,28},{12,0},{16,4},{20,8},{24,12},{28,16},{1,21},{... | collective-permute-start | bytes 589832 | tf_op jit(solution)/shard_map/ppermute | solution.py:123
  355.4 26.9 %collective-permute-start.21 = (f32[1,3,16,16,64]{4,3,2,0,1:T(8,128)S(1)}, f32[1,3,16,16,64]{4,3,2,0,1:T(8,128)S(1)}, u32[]{:S(2)}, u32[]{:S(2)}) collective-permute-start(f32[1,3,16,16,64]{4,3,2,0,1:T(8,128)S(1)} %get-tuple-element.46), channel_id=1, source_target_pairs={{0,12},{4,16},{8,20},{12,24},{16,28},{20,0},{24,4},{28,8},{1,13},{... | collective-permute-start | bytes 589832 | tf_op jit(solution)/shard_map/ppermute | solution.py:123
  364.8 23.3 %collective-permute-start.22 = (f32[1,3,16,16,64]{4,3,2,0,1:T(8,128)S(1)}, f32[1,3,16,16,64]{4,3,2,0,1:T(8,128)S(1)}, u32[]{:S(2)}, u32[]{:S(2)}) collective-permute-start(f32[1,3,16,16,64]{4,3,2,0,1:T(8,128)S(1)} %get-tuple-element.45), channel_id=1, source_target_pairs={{0,16},{4,20},{8,24},{12,28},{16,0},{20,4},{24,8},{28,12},{1,17},{... | collective-permute-start | bytes 589832 | tf_op jit(solution)/shard_map/ppermute | solution.py:123
  438.7 21.7 %copy-start.6 = (f32[3,16,16,512]{3,2,1,0:T(8,128)}, f32[3,16,16,512]{3,2,1,0:T(8,128)S(1)}, u32[]{:S(2)}) copy-start(f32[3,16,16,512]{3,2,1,0:T(8,128)S(1)} %all_to_all.33) | copy-start | bytes 4718596
  438.8 5.5 %collective-permute-start.26 = (f32[3,1,16,512]{3,2,1,0:T(8,128)S(1)}, f32[3,1,16,512]{3,2,1,0:T(8,128)S(1)}, u32[]{:S(2)}, u32[]{:S(2)}) collective-permute-start(f32[3,1,16,512]{3,2,1,0:T(8,128)S(1)} %get-tuple-element.70), channel_id=1, source_target_pairs={{0,4},{4,8},{8,12},{12,16},{16,20},{20,24},{24,28},{1,5},{5,9},{9,... | collective-permute-start | bytes 294920 | tf_op jit(solution)/shard_map/ppermute | solution.py:32
  442.3 6.8 %collective-permute-start.27 = (f32[3,1,16,512]{3,2,1,0:T(8,128)S(1)}, f32[3,1,16,512]{3,2,1,0:T(8,128)S(1)}, u32[]{:S(2)}, u32[]{:S(2)}) collective-permute-start(f32[3,1,16,512]{3,2,1,0:T(8,128)S(1)} %get-tuple-element.69), channel_id=1, source_target_pairs={{4,0},{8,4},{12,8},{16,12},{20,16},{24,20},{28,24},{5,1},{9,5},{13... | collective-permute-start | bytes 294920 | tf_op jit(solution)/shard_map/ppermute | solution.py:34
  449.4 5.9 %collective-permute-start.28 = (f32[3,18,1,512]{3,2,1,0:T(1,128)S(1)}, f32[3,18,1,512]{3,2,1,0:T(1,128)S(1)}, u32[]{:S(2)}, u32[]{:S(2)}) collective-permute-start(f32[3,18,1,512]{3,2,1,0:T(1,128)S(1)} %get-tuple-element.63), channel_id=1, source_target_pairs={{0,1},{1,2},{2,3},{4,5},{5,6},{6,7},{8,9},{9,10},{10,11},{12,13},{... | collective-permute-start | bytes 331784 | tf_op jit(solution)/shard_map/ppermute | solution.py:32
  453.1 5.5 %collective-permute-start.29 = (f32[3,18,1,512]{3,2,1,0:T(1,128)S(1)}, f32[3,18,1,512]{3,2,1,0:T(1,128)S(1)}, u32[]{:S(2)}, u32[]{:S(2)}) collective-permute-start(f32[3,18,1,512]{3,2,1,0:T(1,128)S(1)} %get-tuple-element.64), channel_id=1, source_target_pairs={{1,0},{2,1},{3,2},{5,4},{6,5},{7,6},{9,8},{10,9},{11,10},{13,12},{... | collective-permute-start | bytes 331784 | tf_op jit(solution)/shard_map/ppermute | solution.py:34
  (16 other events, 28.0 us)
Sparse Core Ops, SparseCore 0:
  40.5 43.2 all-gather.4
  280.0 41.7 all-gather.6
